TPU v7x, 128 devices: a whole 4x4x4 slice. The times are simulated.
128 devices in a mesh: tm: 4 (over x_lo, core), row: 32 (over y, z, x_hi).
Axes of the slice: x: 4 (x_hi: 2, x_lo: 2; x = x_hi * 2 + x_lo), y: 4, z: 4, core: 2. Of those that a mesh axis runs over, the one named last changes fastest.
Arguments:
- queries: bfloat16 [8, 64, 56, 5120], P('tm', 'row'), may hold values from -145 to 145
- frame_keys: bfloat16 [8, 64, 56, 5120], P('tm', 'row'), may hold values from -6.5 to 6.5
- frame_values: bfloat16 [8, 64, 56, 5120], P('tm', 'row'), may hold values from -6 to 6
- tile_mask: int32 [8, 64], P('tm', 'row'), may hold values 0 or 1
- memory_keys: bfloat16 [20, 64, 56, 5120], P('tm', 'row'), may hold values from -6.5 to 6.5
- memory_values: bfloat16 [20, 64, 56, 5120], P('tm', 'row'), may hold values from -6 to 6
- store_slot: int32 [20], replicated, may hold values from 0 to 19, as said below
- retrieved: int32 [8, 2], replicated, may hold values from 0 to 19, as said below
- valid_count: int32 [8], replicated, may hold values from 1 to 2
Outputs:
- attended: bfloat16 [8, 64, 56, 5120], P('tm', 'row')
Inputs may be any that keep to these rules, and one draw needn't show every extreme that they name: `store_slot`: each store position appears once. `retrieved`: for each time slab of 2 consecutive frames, at most 2 of its 4 list entries (padded ones included) name frames whose store positions lie in one aligned block 5t to 5t+4 (the positions of one owner along tm), and in every slab some such block is named exactly 2 times.
All inputs are finite; a program needn't handle non-finite values. No bound on the sum of `tile_mask` on one device may be relied on, other than what follows from the above.
Results may differ from a plain program's by a relative error of at most 0.0033.
Values may be sent and summed in bfloat16 or wider, within the bound.
No kernel may reach another device: no remote copies, remote signals or barrier semaphores. Data moves between devices by JAX's collectives and lax.ppermute only.
A program may use at most 192 MiB of HBM per device.

v0:
```python
import jax
import jax.numpy as jnp
from jax import lax
from jax.sharding import PartitionSpec as P

HD = 128
CW = 8
MR = 1
MEM_K = 2
CAP = 2


def with_halo(cells, sides, width):
    for axis, dim in sides:
        count = lax.axis_size(axis)
        ends = count - 1
        head = lax.slice_in_dim(cells, 0, width, axis=dim)
        tail = lax.slice_in_dim(cells, cells.shape[dim] - width, cells.shape[dim], axis=dim)
        cells = jnp.concatenate(
            [
                lax.ppermute(tail, axis, [(i, (i + 1) % count) for i in range(ends)]),
                cells,
                lax.ppermute(head, axis, [((i + 1) % count, i) for i in range(ends)]),
            ],
            axis=dim,
        )
    return cells


def attend_heads(query_rows, key_rows, value_rows, allowed, head_group):
    head_count = query_rows.shape[1]
    block_count = head_count // head_group

    def head_block(block_no):
        start = block_no * head_group
        query_part = lax.dynamic_slice_in_dim(query_rows, start, head_group, 1)
        key_part = lax.dynamic_slice_in_dim(key_rows, start, head_group, 1)
        value_part = lax.dynamic_slice_in_dim(value_rows, start, head_group, 1)
        scores = jnp.einsum(
            "qhd,khd->hqk", query_part, key_part, preferred_element_type=jnp.float32
        ) * HD ** (-0.5)
        scores = jnp.where(allowed[None], scores, -1e30)
        row_top = jnp.max(scores, axis=-1, keepdims=True)
        raised = jnp.exp(scores - row_top)
        row_total = jnp.sum(raised, axis=-1)
        weights = raised.astype(jnp.bfloat16)
        summed = jnp.einsum("hqk,khd->qhd", weights, value_part, preferred_element_type=jnp.float32)
        return summed / jnp.transpose(row_total)[:, :, None]

    blocks = lax.map(head_block, jnp.arange(block_count, dtype=jnp.int32))
    return jnp.transpose(blocks, (1, 0, 2, 3)).reshape(query_rows.shape[0], head_count * HD)


def local(
    queries,
    frame_keys,
    frame_values,
    tile_mask,
    memory_keys,
    memory_values,
    store_slot,
    retrieved,
    valid_count,
):
    frames, row_count, columns, width = queries.shape
    head_count = width // HD
    head_group = 8
    slab_no = lax.axis_index("tm")
    slab_count = lax.axis_size("tm")
    band_no = lax.axis_index("row")
    total_rows = row_count * lax.axis_size("row")
    stored = memory_keys.shape[0]
    entries = frames * MEM_K
    band_size = row_count * columns
    span = row_count + 2 * MR
    mask_float = tile_mask.astype(jnp.bfloat16)
    wide_k = with_halo(frame_keys, (("tm", 0), ("row", 1)), 1)
    wide_v = with_halo(frame_values, (("tm", 0), ("row", 1)), 1)
    wide_mask = with_halo(mask_float, (("tm", 0), ("row", 1)), 1)
    query_frame = jnp.repeat(jnp.arange(frames), band_size)
    query_row = jnp.tile(jnp.repeat(jnp.arange(row_count), columns), frames)
    query_col = jnp.tile(jnp.arange(columns), frames * row_count)
    key_frame = jnp.repeat(jnp.arange(frames + 2) - 1, (row_count + 2) * columns)
    key_row = jnp.tile(jnp.repeat(jnp.arange(row_count + 2) - 1, columns), frames + 2)
    key_col = jnp.tile(jnp.arange(columns), (frames + 2) * (row_count + 2))
    tile_open = jnp.repeat(wide_mask.reshape(-1) == 1, columns)
    nearby = (
        (jnp.abs(key_frame[None] - query_frame[:, None]) <= 1)
        & (jnp.abs(key_row[None] - query_row[:, None]) <= 1)
        & (jnp.abs(key_col[None] - query_col[:, None]) <= CW)
    )
    own_tile = (key_frame[None] == query_frame[:, None]) & (key_row[None] == query_row[:, None])
    allowed = nearby & (tile_open[None] | own_tile)
    self_out = attend_heads(
        queries.reshape(-1, head_count, HD),
        wide_k.reshape(-1, head_count, HD),
        wide_v.reshape(-1, head_count, HD),
        allowed,
        head_group,
    )
    id_table = jnp.arange(store_slot.shape[0], dtype=jnp.int32)
    id_hits = retrieved[:, :, None] == id_table[None, None, :]
    position = jnp.sum(jnp.where(id_hits, store_slot[None, None, :], 0), axis=-1)
    owner_of = (position // stored).reshape(slab_count, entries)
    local_of = (position % stored).reshape(slab_count, entries)
    entry_ids = jnp.arange(entries)
    earlier = entry_ids[None, :] < entry_ids[:, None]
    rank_of = jnp.sum((owner_of[:, :, None] == owner_of[:, None, :]) & earlier[None], axis=-1)
    chosen = (owner_of == slab_no)[:, None, :] & (
        rank_of[:, None, :] == jnp.arange(CAP)[None, :, None]
    )
    picked = jnp.sum(jnp.where(chosen, local_of[:, None, :], 0), axis=-1)
    outgoing_k = memory_keys[picked]
    outgoing_v = memory_values[picked]
    incoming_k = lax.all_to_all(outgoing_k, "tm", split_axis=0, concat_axis=0, tiled=True)
    incoming_v = lax.all_to_all(outgoing_v, "tm", split_axis=0, concat_axis=0, tiled=True)
    mine_owner = lax.dynamic_index_in_dim(owner_of, slab_no, 0, keepdims=False)
    mine_rank = lax.dynamic_index_in_dim(rank_of, slab_no, 0, keepdims=False)
    source = mine_owner * CAP + mine_rank
    fetched_k = incoming_k.reshape(slab_count * CAP, row_count, columns, width)[source]
    fetched_v = incoming_v.reshape(slab_count * CAP, row_count, columns, width)[source]
    fetched_k, fetched_v = (fetched_k, fetched_v)
    wide_k = with_halo(fetched_k, (("row", 1),), MR)
    wide_v = with_halo(fetched_v, (("row", 1),), MR)
    live_counts = lax.dynamic_slice_in_dim(valid_count, slab_no * frames, frames)
    key_row = band_no * row_count - MR + jnp.arange(span)
    query_row = band_no * row_count + jnp.arange(row_count)
    row_ok = (
        (jnp.abs(key_row[None, :] - query_row[:, None]) <= MR)
        & (key_row >= 0)[None, :]
        & (key_row < total_rows)[None, :]
    )
    results = []
    for frame_no in range(frames):
        keys_here = wide_k[frame_no * MEM_K : (frame_no + 1) * MEM_K].reshape(-1, head_count, HD)
        values_here = wide_v[frame_no * MEM_K : (frame_no + 1) * MEM_K].reshape(-1, head_count, HD)
        open_entry = jnp.arange(MEM_K) < live_counts[frame_no]
        allowed = row_ok[:, None, None, :, None] & open_entry[None, None, :, None, None]
        allowed = jnp.broadcast_to(allowed, (row_count, columns, MEM_K, span, columns)).reshape(
            band_size, MEM_K * span * columns
        )
        results.append(
            attend_heads(
                queries[frame_no].reshape(band_size, head_count, HD),
                keys_here,
                values_here,
                allowed,
                head_group,
            )
        )
    memory_out = jnp.concatenate(results, 0)
    return (self_out + memory_out).reshape(frames, row_count, columns, width).astype(jnp.bfloat16)


def solution(mesh):
    in_specs = (
        P("tm", "row", None, None),
        P("tm", "row", None, None),
        P("tm", "row", None, None),
        P("tm", "row"),
        P("tm", "row", None, None),
        P("tm", "row", None, None),
        P(),
        P(),
        P(),
    )
    out_specs = P("tm", "row", None, None)
    return jax.shard_map(local, mesh=mesh, in_specs=in_specs, out_specs=out_specs, check_vma=False)
```

profile of v0, /device:TPU:16, one launch (start us, length us, event | category | flops | bytes accessed | tf_op | source)
XLA Modules:
  0.0 797.1 jit_solution(818335890079792216)
XLA Ops:
  2.0 7.5 gather_fusion
  9.5 5.9 all-to-all-start
  19.6 4.6 collective-permute-start.8
  27.0 4.0 collective-permute-start
  41.5 5.1 collective-permute-start.10
  46.6 5.4 collective-permute-start.11
  60.3 8.4 %collective-permute-start.3 = (bf16[4,1,56,5120]{3,2,1,0:T(8,128)(2,1)}, bf16[4,1,56,5120]{3,2,1,0:T(8,128)(2,1)}, u32[]{:S(2)}, u32[]{:S(2)}) collective-permute-start(bf16[4,1,56,5120]{3,2,1,0:T(8,128)(2,1)} %get-tuple-element.321), channel_id=1, source_target_pairs={{1,0},{2,1},{3,2},{4,3},{5,4},{6,5},{7,6},{8,7},{9,8},{10,9},{11,1... | collective-permute-start | bytes 6881288 | tf_op jit(solution)/shard_map/ppermute | solution.py:23
  68.7 7.6 gather_fusion.2
  85.6 114.1 %collective-permute-done.5 = bf16[1,2]{1,0:T(2,128)(2,1)S(1)} collective-permute-done((bf16[1,2]{1,0:T(2,128)(2,1)S(1)}, bf16[1,2]{1,0:T(2,128)(2,1)S(1)}, u32[]{:S(2)}, u32[]{:S(2)}) %collective-permute-start.5) | collective-permute-done | bytes 36 | tf_op jit(solution)/shard_map/ppermute | solution.py:23
  201.7 116.8 %collective-permute-done.6 = bf16[4,1]{1,0:T(4,128)(2,1)S(1)} collective-permute-done((bf16[4,1]{1,0:T(4,128)(2,1)S(1)}, bf16[4,1]{1,0:T(4,128)(2,1)S(1)}, u32[]{:S(2)}, u32[]{:S(2)}) %collective-permute-start.6) | collective-permute-done | bytes 40 | tf_op jit(solution)/shard_map/ppermute | solution.py:21
  320.9 4.6 collective-permute-done.7
  325.9 9.1 %pad_maximum_fusion.1 = bf16[4,4,56,5120]{3,2,1,0:T(8,128)(2,1)} fusion(bf16[4,1,56,5120]{3,2,1,0:T(8,128)(2,1)} %collective-permute-done.11, bf16[4,2,56,5120]{3,2,1,0:T(8,128)(2,1)} %copy-done, bf16[4,1,56,5120]{3,2,1,0:T(8,128)(2,1)} %collective-permute-done.10), kind=kLoop, calls=%fused_computation.81 | loop fusion | flops 9175040 | bytes 18350080 | tf_op jit(solution)/shard_map/concatenate | solution.py:19
  335.0 10.0 %copy.54 = bf16[112,8,40,128]{3,2,1,0:T(8,128)(2,1)} copy(bf16[112,8,40,128]{3,1,2,0:T(8,128)(2,1)} %bitcast.138) | data formatting | bytes 18350080
  345.0 9.1 %pad_maximum_fusion = bf16[4,4,56,5120]{3,2,1,0:T(8,128)(2,1)} fusion(bf16[4,1,56,5120]{3,2,1,0:T(8,128)(2,1)} %collective-permute-done.3, bf16[4,2,56,5120]{3,2,1,0:T(8,128)(2,1)} %copy-done.1, bf16[4,1,56,5120]{3,2,1,0:T(8,128)(2,1)} %collective-permute-done.2), kind=kLoop, calls=%fused_computation.80 | loop fusion | flops 9175040 | bytes 18350080 | tf_op jit(solution)/shard_map/concatenate | solution.py:19
  354.1 9.8 %copy.52 = bf16[112,8,40,128]{3,2,1,0:T(8,128)(2,1)} copy(bf16[112,8,40,128]{3,1,2,0:T(8,128)(2,1)} %bitcast.139) | data formatting | bytes 18350080
  363.9 30.6 %all-to-all-start.1 = ((bf16[4,2,2,56,5120]{4,3,2,1,0:T(8,128)(2,1)}), bf16[4,2,2,56,5120]{4,3,2,1,0:T(8,128)(2,1)}, u32[]{:S(2)}, u32[]{:S(2)}) async-start(bf16[4,2,2,56,5120]{4,3,2,1,0:T(8,128)(2,1)} %bitcast.137), calls=%async_computation.1 | async-start | bytes 18350080 | tf_op jit(solution)/shard_map/all_to_all | solution.py:115
  394.5 6.7 gather_fusion.1
  401.2 4.8 fusion.83
  405.9 3.0 collective-permute-start.12
  408.9 54.3 %while.33 = (s32[]{:T(128)}, f32[5,224,8,128]{3,1,2,0:T(8,128)}, s32[5]{0:T(128)S(1)}, bf16[896,40,128]{2,1,0:T(8,128)(2,1)}, bf16[224,40,128]{2,1,0:T(8,128)(2,...) while((s32[]{:T(128)}, f32[5,224,8,128]{3,1,2,0:T(8,128)}, ...), condition=%wide.region_3.4_spmd.clone, body=%wide.region_0.3_spmd.clone.sunk | while | flops 843182592 | bytes 33425120 | solution.py:50
  416.6 3.2 fusion.113
  427.4 3.2 fusion.113
  438.2 3.2 fusion.113
  449.1 3.2 fusion.113
  460.0 3.2 fusion.113
  463.2 7.1 copy.30
  470.3 5.3 reshape.273
  475.6 7.5 collective-permute-start.13
  483.1 16.1 %all-to-all-done.1 = bf16[4,2,2,56,5120]{4,3,2,1,0:T(8,128)(2,1)} async-done(((bf16[4,2,2,56,5120]{4,3,2,1,0:T(8,128)(2,1)}), bf16[4,2,2,56,5120]{4,3,2,1,0:T(8,128)(2,1)}, u32[]{:S(2)}, u32[]{:S(2)}) %all-to-all-start.1) | async-done | bytes 9175072 | tf_op jit(solution)/shard_map/all_to_all | solution.py:115
  499.2 6.6 gather_fusion.3
  505.8 4.9 fusion.82
  513.6 7.5 collective-permute-start.15
  521.1 27.4 %collective-permute-done.12 = bf16[4,1,56,5120]{3,2,1,0:T(8,128)(2,1)} collective-permute-done((bf16[4,1,56,5120]{3,2,1,0:T(8,128)(2,1)}, bf16[4,1,56,5120]{3,2,1,0:T(8,128)(2,1)}, u32[]{:S(2)}, u32[]{:S(2)}) %collective-permute-start.12) | collective-permute-done | bytes 2293792 | tf_op jit(solution)/shard_map/ppermute | solution.py:21
  548.5 3.1 constant_dynamic-update-slice_fusion.8
  554.2 38.0 %collective-permute-done.13 = bf16[4,1,56,5120]{3,2,1,0:T(8,128)(2,1)} collective-permute-done((bf16[4,1,56,5120]{3,2,1,0:T(8,128)(2,1)S(1)}, bf16[4,1,56,5120]{3,2,1,0:T(8,128)(2,1)}, u32[]{:S(2)}, u32[]{:S(2)}) %collective-permute-start.13) | collective-permute-done | bytes 2293792 | tf_op jit(solution)/shard_map/ppermute | solution.py:23
  592.2 3.2 constant_dynamic-update-slice_fusion.6
  595.4 6.6 fusion.81
  602.1 3.3 copy.59
  605.4 41.5 %collective-permute-done.14 = bf16[4,1,56,5120]{3,2,1,0:T(8,128)(2,1)} collective-permute-done((bf16[4,1,56,5120]{3,2,1,0:T(8,128)(2,1)}, bf16[4,1,56,5120]{3,2,1,0:T(8,128)(2,1)}, u32[]{:S(2)}, u32[]{:S(2)}) %collective-permute-start.14) | collective-permute-done | bytes 2293792 | tf_op jit(solution)/shard_map/ppermute | solution.py:21
  646.8 3.2 constant_dynamic-update-slice_fusion.11
  652.6 37.9 %collective-permute-done.15 = bf16[4,1,56,5120]{3,2,1,0:T(8,128)(2,1)} collective-permute-done((bf16[4,1,56,5120]{3,2,1,0:T(8,128)(2,1)}, bf16[4,1,56,5120]{3,2,1,0:T(8,128)(2,1)}, u32[]{:S(2)}, u32[]{:S(2)}) %collective-permute-start.15) | collective-permute-done | bytes 2293792 | tf_op jit(solution)/shard_map/ppermute | solution.py:23
  690.5 3.2 constant_dynamic-update-slice_fusion.9
  693.7 6.6 fusion.80
  700.3 3.4 copy.61
  705.3 35.0 %while.35 = (s32[]{:T(128)}, f32[5,112,8,128]{3,1,2,0:T(8,128)}, s32[5]{0:T(128)S(1)}, bf16[448,40,128]{2,1,0:T(8,128)(2,1)}, bf16[112,40,128]{2,1,0:T(8,128)(2,...) while((s32[]{:T(128)}, f32[5,112,8,128]{3,1,2,0:T(8,128)}, ...), condition=%wide.region_14.15_spmd.clone, body=%wide.region_11.14_spmd.clone.sunk | while | flops 210049280 | bytes 11788479 | solution.py:50
  744.5 5.8 copy.55
  750.2 3.3 copy.57
  755.2 35.0 %while.34 = (s32[]{:T(128)}, f32[5,112,8,128]{3,1,2,0:T(8,128)}, s32[5]{0:T(128)S(1)}, bf16[448,40,128]{2,1,0:T(8,128)(2,1)}, bf16[112,40,128]{2,1,0:T(8,128)(2,...) while((s32[]{:T(128)}, f32[5,112,8,128]{3,1,2,0:T(8,128)}, ...), condition=%wide.region_10.11_spmd.clone, body=%wide.region_7.10_spmd.clone.sunk | while | flops 210049280 | bytes 11788479 | solution.py:50
  (250 shorter events, 162.3 us)
Async XLA Ops:
  9.5 5.9 copy-start.9
  9.5 8.4 %copy-start.3 = (bf16[2,2,56,5120]{3,2,1,0:T(8,128)(2,1)S(1)}, bf16[2,2,56,5120]{3,2,1,0:T(8,128)(2,1)}, u32[]{:S(2)}) copy-start(bf16[2,2,56,5120]{3,2,1,0:T(8,128)(2,1)} %param.16) | copy-start | bytes 6881284
  9.5 354.4 %all-to-all-start = ((bf16[4,2,2,56,5120]{4,3,2,1,0:T(8,128)(2,1)}), bf16[4,2,2,56,5120]{4,3,2,1,0:T(8,128)(2,1)}, u32[]{:S(2)}, u32[]{:S(2)}) async-start(bf16[4,2,2,56,5120]{4,3,2,1,0:T(8,128)(2,1)} %bitcast.136), calls=%async_computation | async-start | bytes 18350080 | tf_op jit(solution)/shard_map/all_to_all | solution.py:116
  15.5 10.0 %copy-start.4 = (bf16[2,2,56,5120]{3,2,1,0:T(8,128)(2,1)S(1)}, bf16[2,2,56,5120]{3,2,1,0:T(8,128)(2,1)}, u32[]{:S(2)}) copy-start(bf16[2,2,56,5120]{3,2,1,0:T(8,128)(2,1)} %param.17) | copy-start | bytes 6881284
  15.5 68.8 %collective-permute-start.4 = (bf16[1,2]{1,0:T(2,128)(2,1)S(1)}, bf16[1,2]{1,0:T(2,128)(2,1)S(1)}, u32[]{:S(2)}, u32[]{:S(2)}) collective-permute-start(bf16[1,2]{1,0:T(2,128)(2,1)S(1)} %get-tuple-element.336), channel_id=1, source_target_pairs={{0,32},{32,64},{64,96},{1,33},{33,65},{65,97},{2,34},{34,66},{66,9... | collective-permute-start | bytes 20 | tf_op jit(solution)/shard_map/ppermute | solution.py:21
  19.6 15.6 %collective-permute-start.8 = (bf16[1,2,56,5120]{3,2,1,0:T(8,128)(2,1)}, bf16[1,2,56,5120]{3,2,1,0:T(8,128)(2,1)}, u32[]{:S(2)}, u32[]{:S(2)}) collective-permute-start(bf16[1,2,56,5120]{3,2,1,0:T(8,128)(2,1)} %get-tuple-element.325), channel_id=1, source_target_pairs={{0,32},{32,64},{64,96},{1,33},{33,65},{65,97},{2,34},{34,66},{66,9... | collective-permute-start | bytes 3440648 | tf_op jit(solution)/shard_map/ppermute | solution.py:21
  24.2 12.5 %collective-permute-start.9 = (bf16[1,2,56,5120]{3,2,1,0:T(8,128)(2,1)}, bf16[1,2,56,5120]{3,2,1,0:T(8,128)(2,1)}, u32[]{:S(2)}, u32[]{:S(2)}) collective-permute-start(bf16[1,2,56,5120]{3,2,1,0:T(8,128)(2,1)} %get-tuple-element.324), channel_id=1, source_target_pairs={{32,0},{64,32},{96,64},{33,1},{65,33},{97,65},{34,2},{66,34},{98,6... | collective-permute-start | bytes 3440648 | tf_op jit(solution)/shard_map/ppermute | solution.py:23
  27.0 25.0 %collective-permute-start = (bf16[1,2,56,5120]{3,2,1,0:T(8,128)(2,1)}, bf16[1,2,56,5120]{3,2,1,0:T(8,128)(2,1)}, u32[]{:S(2)}, u32[]{:S(2)}) collective-permute-start(bf16[1,2,56,5120]{3,2,1,0:T(8,128)(2,1)} %get-tuple-element.327), channel_id=1, source_target_pairs={{0,32},{32,64},{64,96},{1,33},{33,65},{65,97},{2,34},{34,66},{66,9... | collective-permute-start | bytes 3440648 | tf_op jit(solution)/shard_map/ppermute | solution.py:21
  31.1 22.4 %collective-permute-start.1 = (bf16[1,2,56,5120]{3,2,1,0:T(8,128)(2,1)}, bf16[1,2,56,5120]{3,2,1,0:T(8,128)(2,1)}, u32[]{:S(2)}, u32[]{:S(2)}) collective-permute-start(bf16[1,2,56,5120]{3,2,1,0:T(8,128)(2,1)} %get-tuple-element.326), channel_id=1, source_target_pairs={{32,0},{64,32},{96,64},{33,1},{65,33},{97,65},{34,2},{66,34},{98,6... | collective-permute-start | bytes 3440648 | tf_op jit(solution)/shard_map/ppermute | solution.py:23
  38.1 3.4 copy-start
  41.5 11.8 %copy-start.5 = (bf16[2,2,56,5120]{3,2,1,0:T(8,128)(2,1)S(1)}, bf16[2,2,56,5120]{3,2,1,0:T(8,128)(2,1)}, u32[]{:S(2)}) copy-start(bf16[2,2,56,5120]{3,2,1,0:T(8,128)(2,1)} %param.17) | copy-start | bytes 6881284
  41.5 284.4 %collective-permute-start.10 = (bf16[4,1,56,5120]{3,2,1,0:T(8,128)(2,1)}, bf16[4,1,56,5120]{3,2,1,0:T(8,128)(2,1)}, u32[]{:S(2)}, u32[]{:S(2)}) collective-permute-start(bf16[4,1,56,5120]{3,2,1,0:T(8,128)(2,1)} %get-tuple-element.318), channel_id=1, source_target_pairs={{0,1},{1,2},{2,3},{3,4},{4,5},{5,6},{6,7},{7,8},{8,9},{9,10},{10,1... | collective-permute-start | bytes 6881288 | tf_op jit(solution)/shard_map/ppermute | solution.py:21
  46.6 279.3 %collective-permute-start.11 = (bf16[4,1,56,5120]{3,2,1,0:T(8,128)(2,1)}, bf16[4,1,56,5120]{3,2,1,0:T(8,128)(2,1)}, u32[]{:S(2)}, u32[]{:S(2)}) collective-permute-start(bf16[4,1,56,5120]{3,2,1,0:T(8,128)(2,1)} %get-tuple-element.319), channel_id=1, source_target_pairs={{1,0},{2,1},{3,2},{4,3},{5,4},{6,5},{7,6},{8,7},{9,8},{10,9},{11,1... | collective-permute-start | bytes 6881288 | tf_op jit(solution)/shard_map/ppermute | solution.py:23
  54.9 3.5 copy-start.1
  58.4 286.6 %collective-permute-start.2 = (bf16[4,1,56,5120]{3,2,1,0:T(8,128)(2,1)}, bf16[4,1,56,5120]{3,2,1,0:T(8,128)(2,1)}, u32[]{:S(2)}, u32[]{:S(2)}) collective-permute-start(bf16[4,1,56,5120]{3,2,1,0:T(8,128)(2,1)} %get-tuple-element.320), channel_id=1, source_target_pairs={{0,1},{1,2},{2,3},{3,4},{4,5},{5,6},{6,7},{7,8},{8,9},{9,10},{10,1... | collective-permute-start | bytes 6881288 | tf_op jit(solution)/shard_map/ppermute | solution.py:21
  60.3 284.7 %collective-permute-start.3 = (bf16[4,1,56,5120]{3,2,1,0:T(8,128)(2,1)}, bf16[4,1,56,5120]{3,2,1,0:T(8,128)(2,1)}, u32[]{:S(2)}, u32[]{:S(2)}) collective-permute-start(bf16[4,1,56,5120]{3,2,1,0:T(8,128)(2,1)} %get-tuple-element.321), channel_id=1, source_target_pairs={{1,0},{2,1},{3,2},{4,3},{5,4},{6,5},{7,6},{8,7},{9,8},{10,9},{11,1... | collective-permute-start | bytes 6881288 | tf_op jit(solution)/shard_map/ppermute | solution.py:23
  68.7 7.6 copy-start.6
  79.1 2.5 copy-start.10
  84.3 115.4 %collective-permute-start.5 = (bf16[1,2]{1,0:T(2,128)(2,1)S(1)}, bf16[1,2]{1,0:T(2,128)(2,1)S(1)}, u32[]{:S(2)}, u32[]{:S(2)}) collective-permute-start(bf16[1,2]{1,0:T(2,128)(2,1)S(1)} %get-tuple-element.337), channel_id=1, source_target_pairs={{32,0},{64,32},{96,64},{33,1},{65,33},{97,65},{34,2},{66,34},{98,6... | collective-permute-start | bytes 20 | tf_op jit(solution)/shard_map/ppermute | solution.py:23
  199.8 118.7 %collective-permute-start.6 = (bf16[4,1]{1,0:T(4,128)(2,1)S(1)}, bf16[4,1]{1,0:T(4,128)(2,1)S(1)}, u32[]{:S(2)}, u32[]{:S(2)}) collective-permute-start(bf16[4,1]{1,0:T(4,128)(2,1)S(1)} %get-tuple-element.330), channel_id=1, source_target_pairs={{0,1},{1,2},{2,3},{3,4},{4,5},{5,6},{6,7},{7,8},{8,9},{9,10},{10,1... | collective-permute-start | bytes 32 | tf_op jit(solution)/shard_map/ppermute | solution.py:21
  318.5 7.0 collective-permute-start.7
  363.9 135.3 %all-to-all-start.1 = ((bf16[4,2,2,56,5120]{4,3,2,1,0:T(8,128)(2,1)}), bf16[4,2,2,56,5120]{4,3,2,1,0:T(8,128)(2,1)}, u32[]{:S(2)}, u32[]{:S(2)}) async-start(bf16[4,2,2,56,5120]{4,3,2,1,0:T(8,128)(2,1)} %bitcast.137), calls=%async_computation.1 | async-start | bytes 18350080 | tf_op jit(solution)/shard_map/all_to_all | solution.py:115
  405.9 142.6 %collective-permute-start.12 = (bf16[4,1,56,5120]{3,2,1,0:T(8,128)(2,1)}, bf16[4,1,56,5120]{3,2,1,0:T(8,128)(2,1)}, u32[]{:S(2)}, u32[]{:S(2)}) collective-permute-start(bf16[4,1,56,5120]{3,2,1,0:T(8,128)(2,1)} %get-tuple-element.317), channel_id=1, source_target_pairs={{0,1},{1,2},{2,3},{3,4},{4,5},{5,6},{6,7},{7,8},{8,9},{9,10},{10,1... | collective-permute-start | bytes 6881288 | tf_op jit(solution)/shard_map/ppermute | solution.py:21
  470.3 5.3 copy-start.7
  475.6 116.6 %collective-permute-start.13 = (bf16[4,1,56,5120]{3,2,1,0:T(8,128)(2,1)S(1)}, bf16[4,1,56,5120]{3,2,1,0:T(8,128)(2,1)}, u32[]{:S(2)}, u32[]{:S(2)}) collective-permute-start(bf16[4,1,56,5120]{3,2,1,0:T(8,128)(2,1)S(1)} %copy-done.7), channel_id=1, source_target_pairs={{1,0},{2,1},{3,2},{4,3},{5,4},{6,5},{7,6},{8,7},{9,8},{10,9},{11,1... | collective-permute-start | bytes 6881288 | tf_op jit(solution)/shard_map/ppermute | solution.py:23
  499.2 52.5 %slice-start = ((s8[4587520]{0:T(1024)(128)(4,1)}), s8[393216]{0:T(1024)(128)(4,1)S(1)}, s32[]{:S(2)}) async-start(s8[4587520]{0:T(1024)(128)(4,1)} %bitcast.132), calls=%async_computation.2 | async-start | bytes 786432
  505.8 45.9 %slice-start.1 = ((s8[4587520]{0:T(1024)(128)(4,1)}), s8[4194304]{0:T(1024)(128)(4,1)S(1)}, s32[]{:S(2)}) async-start(s8[4587520]{0:T(1024)(128)(4,1)} %bitcast.132), calls=%async_computation.3 | async-start | bytes 8388608
  510.8 136.1 %collective-permute-start.14 = (bf16[4,1,56,5120]{3,2,1,0:T(8,128)(2,1)}, bf16[4,1,56,5120]{3,2,1,0:T(8,128)(2,1)}, u32[]{:S(2)}, u32[]{:S(2)}) collective-permute-start(bf16[4,1,56,5120]{3,2,1,0:T(8,128)(2,1)} %get-tuple-element.315), channel_id=1, source_target_pairs={{0,1},{1,2},{2,3},{3,4},{4,5},{5,6},{6,7},{7,8},{8,9},{9,10},{10,1... | collective-permute-start | bytes 6881288 | tf_op jit(solution)/shard_map/ppermute | solution.py:21
  513.6 176.9 %collective-permute-start.15 = (bf16[4,1,56,5120]{3,2,1,0:T(8,128)(2,1)}, bf16[4,1,56,5120]{3,2,1,0:T(8,128)(2,1)}, u32[]{:S(2)}, u32[]{:S(2)}) collective-permute-start(bf16[4,1,56,5120]{3,2,1,0:T(8,128)(2,1)} %get-tuple-element.314), channel_id=1, source_target_pairs={{1,0},{2,1},{3,2},{4,3},{5,4},{6,5},{7,6},{8,7},{9,8},{10,9},{11,1... | collective-permute-start | bytes 6881288 | tf_op jit(solution)/shard_map/ppermute | solution.py:23
  602.0 48.0 %slice-start.2 = ((s8[4587520]{0:T(1024)(128)(4,1)}), s8[4194304]{0:T(1024)(128)(4,1)S(1)}, s32[]{:S(2)}) async-start(s8[4587520]{0:T(1024)(128)(4,1)} %bitcast.134), calls=%async_computation.4 | async-start | bytes 8388608
  602.1 48.0 %slice-start.3 = ((s8[4587520]{0:T(1024)(128)(4,1)}), s8[393216]{0:T(1024)(128)(4,1)S(1)}, s32[]{:S(2)}) async-start(s8[4587520]{0:T(1024)(128)(4,1)} %bitcast.134), calls=%async_computation.5 | async-start | bytes 786432
  744.5 5.8 slice-start.6
  744.5 5.8 slice-start.7
  753.6 1.7 copy-start.8
  790.2 3.0 copy-start.2
  792.8 2.2 slice-start.4
  793.2 1.9 slice-start.5
where the time goes:
time: 803 us; the launch traced here: 797 us
  waiting for transfers between devices  396 us (49%)
  local copies, waits for them, and re-layouts  205 us (26%)
  starting transfers between devices  97.4 us (12%)
  matrix products  46.6 us (6%)
  other arithmetic  42.2 us (5%)
  loops' own time  9.52 us (1%)
    ppermute x8, waiting for transfers between devices, with_halo(): lax.ppermute(head, axis, [((i + 1) % count, i) for i in range(ends)])  195 us
    ppermute x8, waiting for transfers between devices, with_halo(): lax.ppermute(tail, axis, [(i, (i + 1) % count) for i in range(ends)])  186 us
    unnamed x57, local copies, waits for them, and re-layouts  60 us
    ppermute x8, starting transfers between devices, with_halo(): lax.ppermute(head, axis, [((i + 1) % count, i) for i in range(ends)])  35.2 us
    dot_general x15, matrix products, head_block(): jnp.einsum('hqk,khd->qhd', weights, value_part, preferred_element_type=jn...  31.7 us
    all_to_all x1, starting transfers between devices, local(): lax.all_to_all(outgoing_k, 'tm', split_axis=0, concat_axis=0, tiled=True)  30.6 us
    dynamic_slice x15, local copies, waits for them, and re-layouts, head_block(): key_part = lax.dynamic_slice_in_dim(key_rows, start, head_group, 1)  27.5 us
    ppermute x8, starting transfers between devices, with_halo(): lax.ppermute(tail, axis, [(i, (i + 1) % count) for i in range(ends)])  25.8 us
  transfers between devices with their start and end apart: 18, of which 8 were waited for; matrix products, arithmetic and copies ran while one was open for 23% of the time, Pallas kernels for 0%

commit v1 on v0

v1 whole, which is shorter than its diff:
```python
import functools
import math

import jax
import jax.numpy as jnp
import numpy as np
from jax import lax
from jax.experimental import pallas as pl
from jax.experimental.pallas import tpu as pltpu
from jax.sharding import PartitionSpec as P

HD = 128
CW = 8
MEM_K = 2
SEG = 64
NEG = -1e30
SCALE = HD ** (-0.5) * math.log2(math.e)
AXES = ("tm", "row")
CHUNKS = 2
VMEM = 56 * 1024 * 1024


def biases(columns):
    key_row = np.repeat(np.arange(2), columns)[:, None]
    key_col = np.tile(np.arange(columns), 2)[:, None]
    query_row = np.repeat(np.arange(4) - 1, SEG)[None]
    query_col = np.tile(np.arange(SEG), 4)[None]
    pad = query_col >= columns
    rows_ok = np.abs(key_row - query_row) <= 1
    cols_ok = np.abs(key_col - query_col) <= CW
    window = np.where(rows_ok & (cols_ok | pad), 0.0, NEG).astype(np.float32)
    memory = np.where(rows_ok, 0.0, NEG).astype(np.float32)
    own = (key_row == query_row).astype(np.float32)
    return window, memory, own


def fill_bias(table, sf, slot, window_ref, own_ref, bias_ref):
    closed0 = jnp.where(table[40 + slot * 2] == 1, 0.0, NEG)
    closed1 = jnp.where(table[40 + slot * 2 + 1] == 1, 0.0, NEG)
    same = jnp.where(table[sf * 4 + slot] == 2, 1.0, 0.0)
    half = bias_ref.shape[0] // 2
    row = lax.broadcasted_iota(jnp.int32, bias_ref.shape, 0)
    closed = jnp.where(row < half, closed0, closed1)
    bias_ref[...] = window_ref[...] + jnp.where(own_ref[...] * same > 0.5, 0.0, closed)


def for_slots(table, frame_refs, memory_refs, window_ref, memory_ref, own_ref, bias_ref, work):
    sf = pl.program_id(0)
    for slot in range(4):

        @pl.when(table[sf * 4 + slot] > 0)
        def _(slot=slot):
            fill_bias(table, sf, slot, window_ref, own_ref, bias_ref)
            work([refs[slot // 2] for refs in frame_refs], slot % 2, bias_ref, 0)

    for entry in range(MEM_K):
        for place in range(2):

            @pl.when(table[16 + sf * 2 + entry] == place + 1)
            def _(entry=entry, place=place):
                work([refs[place * 2 + entry] for refs in memory_refs], 0, memory_ref, 2)


def scores_of(k_ref, position, q_ref, bias_ref, lanes):
    s = lax.dot_general(
        k_ref[position, :, lanes],
        q_ref[0, :, lanes],
        (((1,), (1,)), ((), ())),
        preferred_element_type=jnp.float32,
    )
    return s * SCALE + bias_ref[...]


def stats_kernel(table, q_ref, ko, ks, mo0, mo1, ms0, ms1, window_ref, memory_ref, own_ref, st_ref, bias_ref):
    heads = st_ref.shape[2]
    for kind in (0, 2):
        st_ref[0, kind] = jnp.full(st_ref.shape[2:], NEG, jnp.float32)
        st_ref[0, kind + 1] = jnp.zeros(st_ref.shape[2:], jnp.float32)

    def work(refs, position, bias, kind):
        def head(h, carry):
            lanes = pl.ds(pl.multiple_of(h * HD, HD), HD)
            s = scores_of(refs[0], position, q_ref, bias, lanes)
            top_old = st_ref[0, kind, pl.ds(h, 1), :]
            top = jnp.maximum(top_old, jnp.max(s, axis=0, keepdims=True))
            part = jnp.sum(jnp.exp2(s - top), axis=0, keepdims=True)
            kept = st_ref[0, kind + 1, pl.ds(h, 1), :] * jnp.exp2(top_old - top)
            st_ref[0, kind, pl.ds(h, 1), :] = top
            st_ref[0, kind + 1, pl.ds(h, 1), :] = kept + part
            return carry

        lax.fori_loop(0, heads, head, 0, unroll=math.gcd(heads, 5))

    for_slots(table, [(ko, ks)], [(mo0, mo1, ms0, ms1)], window_ref, memory_ref, own_ref, bias_ref, work)


def output_kernel(
    table, q_ref, tot_ref, ko, ks, vo, vs, mo0, mo1, ms0, ms1, wo0, wo1, ws0, ws1,
    window_ref, memory_ref, own_ref, o_ref, acc_ref, bias_ref,
):
    heads = tot_ref.shape[2]
    columns = o_ref.shape[2]
    acc_ref[...] = jnp.zeros(acc_ref.shape, jnp.float32)

    def work(refs, position, bias, kind):
        k_ref, v_ref = refs

        def head(h, carry):
            lanes = pl.ds(pl.multiple_of(h * HD, HD), HD)
            s = scores_of(k_ref, position, q_ref, bias, lanes)
            top = tot_ref[0, kind, pl.ds(h, 1), :]
            total = tot_ref[0, kind + 1, pl.ds(h, 1), :]
            weights = jnp.exp2(s - top).astype(jnp.bfloat16)
            part = lax.dot_general(
                v_ref[position, :, lanes],
                weights,
                (((0,), (0,)), ((), ())),
                preferred_element_type=jnp.float32,
            )
            share = jnp.where(total > 0, 1.0 / total, 0.0)
            acc_ref[h] += part * share
            return carry

        lax.fori_loop(0, heads, head, 0, unroll=math.gcd(heads, 5))

    for_slots(
        table, [(ko, ks), (vo, vs)], [(mo0, mo1, ms0, ms1), (wo0, wo1, ws0, ws1)],
        window_ref, memory_ref, own_ref, bias_ref, work,
    )

    def finish(h, carry):
        lanes = pl.ds(pl.multiple_of(h * HD, HD), HD)
        turned = jnp.transpose(acc_ref[h])
        for piece in range(4):
            o_ref[0, piece, :, lanes] = turned[piece * SEG : piece * SEG + columns]
        return carry

    lax.fori_loop(0, heads, finish, 0, unroll=math.gcd(heads, 2))


def kernel_specs(band, width, chunk):
    query = pl.BlockSpec((1, 4 * SEG, width), lambda sf, t: (sf, 0, 0))
    frame = pl.BlockSpec((2, band, width), lambda sf, t: (0, 0, chunk))
    own = [pl.BlockSpec((1, band, width), lambda sf, t, e=e: (t[24 + sf * 2 + e], 0, chunk)) for e in range(MEM_K)]
    sib = [pl.BlockSpec((1, band, width), lambda sf, t, e=e: (t[32 + sf * 2 + e], 0, chunk)) for e in range(MEM_K)]
    mask = pl.BlockSpec((band, 4 * SEG), lambda sf, t: (0, 0))
    return query, frame, own + sib, [mask] * 3


def stats_call(table, q, ko, ks, mo, ms, masks, chunk, heads):
    band, width = ko.shape[1], heads * HD
    query, frame, memory, mask = kernel_specs(band, width, chunk)
    return pl.pallas_call(
        stats_kernel,
        grid_spec=pltpu.PrefetchScalarGridSpec(
            num_scalar_prefetch=1,
            grid=(4,),
            in_specs=[query, frame, frame, *memory, *mask],
            out_specs=pl.BlockSpec((1, 4, heads, 4 * SEG), lambda sf, t: (sf, 0, 0, 0)),
            scratch_shapes=[pltpu.VMEM((band, 4 * SEG), jnp.float32)],
        ),
        out_shape=jax.ShapeDtypeStruct((4, 4, heads, 4 * SEG), jnp.float32),
        compiler_params=pltpu.CompilerParams(vmem_limit_bytes=VMEM),
        cost_estimate=pl.CostEstimate(
            flops=heads * 10 * 2 * band * 4 * SEG * HD,
            bytes_accessed=32 * band * width * 2,
            transcendentals=heads * 10 * band * 4 * SEG,
        ),
        name="stats",
    )(table, q, ko, ks, mo, mo, ms, ms, *masks)


def output_call(table, q, totals, ko, ks, vo, vs, mo, ms, wo, ws, masks, chunk, heads, columns):
    band, width = ko.shape[1], heads * HD
    query, frame, memory, mask = kernel_specs(band, width, chunk)
    return pl.pallas_call(
        output_kernel,
        grid_spec=pltpu.PrefetchScalarGridSpec(
            num_scalar_prefetch=1,
            grid=(4,),
            in_specs=[
                query,
                pl.BlockSpec((1, 4, heads, 4 * SEG), lambda sf, t: (sf, 0, 0, 0)),
                frame, frame, frame, frame, *memory, *memory, *mask,
            ],
            out_specs=pl.BlockSpec((1, 4, columns, width), lambda sf, t: (sf, 0, 0, 0)),
            scratch_shapes=[
                pltpu.VMEM((heads, HD, 4 * SEG), jnp.float32),
                pltpu.VMEM((band, 4 * SEG), jnp.float32),
            ],
        ),
        out_shape=jax.ShapeDtypeStruct((4, 4, columns, width), jnp.float32),
        compiler_params=pltpu.CompilerParams(vmem_limit_bytes=VMEM),
        cost_estimate=pl.CostEstimate(
            flops=heads * 10 * 4 * band * 4 * SEG * HD,
            bytes_accessed=64 * band * width * 2,
            transcendentals=heads * 10 * band * 4 * SEG,
        ),
        name="output",
    )(table, q, totals, ko, ks, vo, vs, mo, mo, ms, ms, wo, wo, ws, ws, *masks)


def merge(parts):
    kinds = []
    for kind in (0, 2):
        tops = [jnp.where(p[:, kind + 1] > 0, p[:, kind], NEG) for p in parts]
        top = functools.reduce(jnp.maximum, tops)
        total = sum(p[:, kind + 1] * jnp.exp2(t - top) for p, t in zip(parts, tops))
        kinds += [top, total]
    return jnp.stack(kinds, 1)


def local(
    queries,
    frame_keys,
    frame_values,
    tile_mask,
    memory_keys,
    memory_values,
    store_slot,
    retrieved,
    valid_count,
):
    frames, rows, columns, width = queries.shape
    slabs, bands = lax.axis_size("tm"), lax.axis_size("row")
    stored = memory_keys.shape[0]
    band = rows * columns
    heads = width // HD // CHUNKS
    part = heads * HD
    slab = lax.axis_index("tm")

    def pairs(slab_of, step):
        return [
            (t * bands + r, slab_of(t) * bands + r + step)
            for t in range(slabs)
            for r in range(bands)
            if 0 <= r + step < bands
        ]

    def core(x):
        return lax.ppermute(x, AXES, pairs(lambda t: t ^ 1, 0))

    def cross(x):
        return lax.ppermute(x, AXES, pairs(lambda t: t ^ 2, 0))

    def down(x):
        return lax.ppermute(x, AXES, pairs(lambda t: t ^ 2, 1))

    def up(x):
        return lax.ppermute(x, AXES, pairs(lambda t: t ^ 2, -1))

    sib = slab ^ 1
    query_frames = jnp.concatenate([slab * frames + jnp.arange(frames), (slab ^ 2) * frames + jnp.arange(frames)])
    key_frames = jnp.concatenate([slab * frames + jnp.arange(frames), sib * frames + jnp.arange(frames)])
    gap = jnp.abs(query_frames[:, None] - key_frames[None, :])
    seen = jnp.where(gap == 0, 2, jnp.where(gap == 1, 1, 0))
    ids = jnp.arange(store_slot.shape[0], dtype=jnp.int32)
    position = jnp.sum(jnp.where(retrieved[:, :, None] == ids, store_slot, 0), axis=-1)
    live = jnp.arange(MEM_K)[None, :] < valid_count[:, None]
    wanted = query_frames[:, None] == jnp.arange(retrieved.shape[0])[None, :]
    place = jnp.sum(jnp.where(wanted[:, :, None], position[None], 0), axis=1)
    alive = jnp.sum(jnp.where(wanted[:, :, None], live[None].astype(jnp.int32), 0), axis=1) > 0
    owner, spot = place // stored, place % stored
    source = jnp.where(alive & (owner == slab), 1, jnp.where(alive & (owner == sib), 2, 0))
    spot_own = jnp.where(source == 1, spot, 0)
    spot_sib = jnp.where(source == 2, spot, 0)
    open_tiles = jnp.concatenate([tile_mask, core(tile_mask)], 0)
    table = jnp.concatenate(
        [v.reshape(-1).astype(jnp.int32) for v in (seen, source, spot_own, spot_sib, open_tiles)]
    )

    ko, vo = frame_keys.reshape(frames, band, width), frame_values.reshape(frames, band, width)
    mo, wo = memory_keys.reshape(stored, band, width), memory_values.reshape(stored, band, width)
    ks, ms = core(ko), core(mo)
    vs, ws = core(vo), core(wo)
    masks = [jnp.asarray(m) for m in biases(columns)]

    asked = []
    for chunk in range(CHUNKS):
        mine = queries[..., chunk * part : (chunk + 1) * part]
        if chunk % 2 == 0:
            theirs = cross(mine)
            both = jnp.concatenate([mine, theirs], 0)
            above, below = down(both[:, 1]), up(both[:, 0])
            above = jnp.concatenate([above[frames:], above[:frames]], 0)
            below = jnp.concatenate([below[frames:], below[:frames]], 0)
        else:
            above, below = down(mine[:, 1]), up(mine[:, 0])
            moved = cross(jnp.concatenate([mine, above[:, None], below[:, None]], 1))
            both = jnp.concatenate([mine, moved[:, :2]], 0)
            above = jnp.concatenate([moved[:, 2], above], 0)
            below = jnp.concatenate([moved[:, 3], below], 0)
        q = jnp.stack([above, both[:, 0], both[:, 1], below], 1)
        q = jnp.pad(q, ((0, 0), (0, 0), (0, SEG - columns), (0, 0)))
        asked.append(q.reshape(2 * frames, 4 * SEG, part))

    stats = [stats_call(table, asked[c], ko, ks, mo, ms, masks, c, heads) for c in range(CHUNKS)]

    totals = []
    for st in stats:
        from_below, from_above = up(st[..., :SEG]), down(st[..., 3 * SEG :])
        edge = jnp.concatenate([from_above, from_below], -1)
        own = st[..., SEG : 3 * SEG]
        joined = cross(merge([own[frames:], edge[:frames]]))
        total = merge([own[:frames], edge[frames:], joined])
        both = jnp.concatenate([total, cross(total)], 0)
        above, below = down(both[..., SEG:]), up(both[..., :SEG])
        above = jnp.concatenate([above[frames:], above[:frames]], 0)
        below = jnp.concatenate([below[frames:], below[:frames]], 0)
        totals.append(jnp.concatenate([above, both, below], -1))

    results = []
    for c in range(CHUNKS):
        o = output_call(table, asked[c], totals[c], ko, ks, vo, vs, mo, ms, wo, ws, masks, c, heads, columns)
        above, own, below = o[:, 0], o[:, 1:3], o[:, 3]
        sent = jnp.bfloat16
        if c % 2 == 0:
            from_below, from_above = up(above.astype(sent)), down(below.astype(sent))
            edge = jnp.stack([from_above, from_below], 1).astype(jnp.float32)
            joined = cross((own[frames:] + edge[:frames]).astype(sent))
            results.append((own[:frames] + edge[frames:] + joined.astype(jnp.float32)).astype(jnp.bfloat16))
        else:
            moved = cross(
                jnp.concatenate([above[:frames, None], own[frames:], below[:frames, None]], 1).astype(sent)
            )
            from_below = up((above[frames:] + moved[:, 0].astype(jnp.float32)).astype(sent))
            from_above = down((below[frames:] + moved[:, 3].astype(jnp.float32)).astype(sent))
            edge = jnp.stack([from_above, from_below], 1).astype(jnp.float32)
            results.append((own[:frames] + edge + moved[:, 1:3].astype(jnp.float32)).astype(jnp.bfloat16))
    return jnp.concatenate(results, -1)


def solution(mesh):
    in_specs = (
        P("tm", "row", None, None),
        P("tm", "row", None, None),
        P("tm", "row", None, None),
        P("tm", "row"),
        P("tm", "row", None, None),
        P("tm", "row", None, None),
        P(),
        P(),
        P(),
    )
    out_specs = P("tm", "row", None, None)
    return jax.shard_map(local, mesh=mesh, in_specs=in_specs, out_specs=out_specs, check_vma=False)
```

time: 803 us -> 430 us (0.54)
  waiting for transfers between devices: 396 us -> 179 us
  local copies, waits for them, and re-layouts: 205 us -> 21.8 us
  Pallas kernels: 0 us -> 103 us
  matrix products: 46.6 us -> 0 us
  other arithmetic: 42.2 us -> 24 us
  loops' own time: 9.52 us -> 0 us
    ppermute x16 -> x29, waiting for transfers between devices: 380 us -> 179 us  [the longest x8 89.3 us: cross(): return lax.ppermute(x, AXES, pairs(lambda t: t ^ 2, 0))]
    pallas_call x0 -> x4, Pallas kernels: none -> 103 us  [the longest x2 66.8 us: output_call(): pl.pallas_call(output_kernel, grid_spec=pltpu.PrefetchScalarGridSpec(num_...]
    unnamed x57 -> x25, local copies, waits for them, and re-layouts: 60 us -> 2.76 us
    dot_general x30 -> x0, matrix products: 46.6 us -> none  [the longest x15 31.7 us: head_block(): jnp.einsum('hqk,khd->qhd', weights, value_part, preferred_element_type=jn...]
    dynamic_slice x46 -> x0, local copies, waits for them, and re-layouts: 46.3 us -> none  [the longest x15 27.5 us: head_block(): key_part = lax.dynamic_slice_in_dim(key_rows, start, head_group, 1)]
    ppermute x16 -> x29, starting transfers between devices: 61 us -> 101 us  [the longest x8 64.6 us: up(): return lax.ppermute(x, AXES, pairs(lambda t: t ^ 2, -1))]
    all_to_all x2 -> x0, starting transfers between devices: 36.5 us -> none  [the longest x1 30.6 us: local(): lax.all_to_all(outgoing_k, 'tm', split_axis=0, concat_axis=0, tiled=True)]
    gather x4 -> x0, local copies, waits for them, and re-layouts: 28.4 us -> none  [the longest x1 7.55 us: local(): outgoing_k = memory_keys[picked]]
  transfers between devices with their start and end apart: 18 -> 29, of which waited for: 8 -> 13; matrix products, arithmetic and copies ran while one was open for 23% -> 8% of each run, Pallas kernels for 0% -> 16%
where the time goes in v1:
time: 430 us; the launch traced here: 428 us
  waiting for transfers between devices  179 us (42%)
  Pallas kernels  103 us (24%)
  starting transfers between devices  101 us (23%)
  other arithmetic  24 us (6%)
  local copies, waits for them, and re-layouts  21.8 us (5%)
    ppermute x8, waiting for transfers between devices, cross(): return lax.ppermute(x, AXES, pairs(lambda t: t ^ 2, 0))  89.3 us
    pallas_call x2, Pallas kernels, output_call(): pl.pallas_call(output_kernel, grid_spec=pltpu.PrefetchScalarGridSpec(num_...  66.8 us
    ppermute x8, starting transfers between devices, up(): return lax.ppermute(x, AXES, pairs(lambda t: t ^ 2, -1))  64.6 us
    ppermute x8, waiting for transfers between devices, up(): return lax.ppermute(x, AXES, pairs(lambda t: t ^ 2, -1))  44.8 us
    ppermute x8, waiting for transfers between devices, down(): return lax.ppermute(x, AXES, pairs(lambda t: t ^ 2, 1))  44.5 us
    pallas_call x2, Pallas kernels, stats_call(): pl.pallas_call(stats_kernel, grid_spec=pltpu.PrefetchScalarGridSpec(num_s...  35.9 us
    ppermute x8, starting transfers between devices, down(): return lax.ppermute(x, AXES, pairs(lambda t: t ^ 2, 1))  27.2 us
    another operation x4, other arithmetic, local(): q = jnp.stack([above, both[:, 0], both[:, 1], below], 1)  9.16 us
  transfers between devices with their start and end apart: 29, of which 13 were waited for; matrix products, arithmetic and copies ran while one was open for 8% of the time, Pallas kernels for 16%

profile of v1, /device:TPU:16, one launch (start us, length us, event | category | flops | bytes accessed | tf_op | source)
XLA Modules:
  0.0 428.2 jit_solution(14594924787394268295)
XLA Ops:
  0.0 2.5 slice_bitcast_fusion.6
  2.5 4.7 %collective-permute-start.17 = (bf16[2,56,2560]{2,1,0:T(8,128)(2,1)}, bf16[2,56,2560]{2,1,0:T(8,128)(2,1)S(1)}, u32[]{:S(2)}, u32[]{:S(2)}) collective-permute-start(bf16[2,56,2560]{2,1,0:T(8,128)(2,1)} %get-tuple-element.35), channel_id=1, source_target_pairs={{0,65},{1,66},{2,67},{3,68},{4,69},{5,70},{6,71},{7,72},{8,73},{9,... | collective-permute-start | bytes 1720328 | tf_op jit(solution)/shard_map/ppermute | solution.py:247
  7.2 5.4 %collective-permute-start.18 = (bf16[2,56,2560]{2,1,0:T(8,128)(2,1)}, bf16[2,56,2560]{2,1,0:T(8,128)(2,1)}, u32[]{:S(2)}, u32[]{:S(2)}) collective-permute-start(bf16[2,56,2560]{2,1,0:T(8,128)(2,1)} %get-tuple-element.36), channel_id=1, source_target_pairs={{1,64},{2,65},{3,66},{4,67},{5,68},{6,69},{7,70},{8,71},{9,72},{10... | collective-permute-start | bytes 1720328 | tf_op jit(solution)/shard_map/ppermute | solution.py:250
  12.7 3.2 fusion.63
  17.7 26.3 %collective-permute-done.1 = bf16[2,2,56,2560]{3,2,1,0:T(8,128)(2,1)} collective-permute-done((bf16[2,2,56,2560]{3,2,1,0:T(8,128)(2,1)}, bf16[2,2,56,2560]{3,2,1,0:T(8,128)(2,1)}, u32[]{:S(2)}, u32[]{:S(2)}) %collective-permute-start.1) | collective-permute-done | bytes 1146912 | tf_op jit(solution)/shard_map/ppermute | solution.py:244
  43.9 3.2 fusion.20
  47.1 1.9 collective-permute-start.2
  50.5 8.1 %collective-permute-start.3 = (bf16[4,56,2560]{2,1,0:T(8,128)(2,1)}, bf16[4,56,2560]{2,1,0:T(8,128)(2,1)S(1)}, u32[]{:S(2)}, u32[]{:S(2)}) collective-permute-start(bf16[4,56,2560]{2,1,0:T(8,128)(2,1)} %get-tuple-element.30), channel_id=1, source_target_pairs={{1,64},{2,65},{3,66},{4,67},{5,68},{6,69},{7,70},{8,71},{9,72},{10... | collective-permute-start | bytes 3440648 | tf_op jit(solution)/shard_map/ppermute | solution.py:250
  58.6 1.6 pad_maximum_fusion
  60.3 21.4 %collective-permute-done.2 = bf16[4,56,2560]{2,1,0:T(8,128)(2,1)} collective-permute-done((bf16[4,56,2560]{2,1,0:T(8,128)(2,1)}, bf16[4,56,2560]{2,1,0:T(8,128)(2,1)}, u32[]{:S(2)}, u32[]{:S(2)}) %collective-permute-start.2) | collective-permute-done | bytes 1146912 | tf_op jit(solution)/shard_map/ppermute | solution.py:247
  83.0 18.1 %collective-permute-done.3 = bf16[4,56,2560]{2,1,0:T(8,128)(2,1)S(1)} collective-permute-done((bf16[4,56,2560]{2,1,0:T(8,128)(2,1)}, bf16[4,56,2560]{2,1,0:T(8,128)(2,1)S(1)}, u32[]{:S(2)}, u32[]{:S(2)}) %collective-permute-start.3) | collective-permute-done | bytes 1146912 | tf_op jit(solution)/shard_map/ppermute | solution.py:250
  101.4 4.5 %fusion.9 = bf16[4,4,64,2560]{3,2,1,0:T(8,128)(2,1)} fusion(bf16[4,1,56,2560]{3,2,1,0:T(8,128)(2,1)S(1)} %get-tuple-element.76, bf16[4,1,56,2560]{3,2,1,0:T(8,128)(2,1)S(1)} %get-tuple-element.75, bf16[2,2,56,2560]{3,2,1,0:T(8,128)(2,1)} %collective-permute-done.1, bf16[2,2,56,2560]{3,2,1,0:T(8,128)(2,1)} %get-tuple-element.31), kind=kLoop, calls=%fused_computation.10 | loop fusion | flops 34078720 | bytes 9830400 | tf_op jit(solution)/shard_map/stack | solution.py:293
  105.9 45.7 %collective-permute-done.19 = bf16[2,4,56,2560]{3,2,0,1:T(8,128)(2,1)S(1)} collective-permute-done((bf16[2,4,56,2560]{3,2,0,1:T(8,128)(2,1)S(1)}, bf16[2,4,56,2560]{3,2,0,1:T(8,128)(2,1)S(1)}, u32[]{:S(2)}, u32[]{:S(2)}) %collective-permute-start.19) | collective-permute-done | bytes 2293792 | tf_op jit(solution)/shard_map/ppermute | solution.py:244
  151.8 1.4 maximum_bitcast_fusion.2
  153.2 3.1 fusion.12
  156.3 17.9 %stats.3 = f32[4,4,20,256]{3,2,1,0:T(8,128)} custom-call(s32[48]{0:T(128)} %concatenate.73.table, bf16[4,256,2560]{2,1,0:T(8,128)(2,1)} %bitcast.71, bf16[2,112,5120]{2,1,0:T(8,128)(2,1)} %bitcast.73, bf16[2,112,5120]{2,1,0:T(8,128)(2,1)} %collective-permute-done.4.ks, bf16[5,112,5120]{2,1,0:T(8,128)(2,1)} %bitcast.56, bf16[5,112,5120]{2,1,0:T(8,128)(2,1)} %bitcast.57, ...), custom_call_target="tpu_custom_call" | custom-call | flops 1468006400 | bytes 18350080 | tf_op jit(solution)/shard_map/stats/pallas_call | solution.py:153
  175.4 7.0 %collective-permute-start.20 = (f32[4,4,20,64]{3,2,1,0:T(8,128)S(1)}, f32[4,4,20,64]{3,2,1,0:T(8,128)S(1)}, u32[]{:S(2)}, u32[]{:S(2)}) collective-permute-start(f32[4,4,20,64]{3,2,1,0:T(8,128)S(1)} %get-tuple-element.54), channel_id=1, source_target_pairs={{0,65},{1,66},{2,67},{3,68},{4,69},{5,70},{6,71},{7,72},{8,73},{9,... | collective-permute-start | bytes 245768 | tf_op jit(solution)/shard_map/ppermute | solution.py:247
  182.4 4.4 %collective-permute-start.21 = (f32[4,4,20,64]{3,2,1,0:T(8,128)S(1)}, f32[4,4,20,64]{3,2,1,0:T(8,128)S(1)}, u32[]{:S(2)}, u32[]{:S(2)}) collective-permute-start(f32[4,4,20,64]{3,2,1,0:T(8,128)S(1)} %get-tuple-element.53), channel_id=1, source_target_pairs={{1,64},{2,65},{3,66},{4,67},{5,68},{6,69},{7,70},{8,71},{9,72},{10... | collective-permute-start | bytes 245768 | tf_op jit(solution)/shard_map/ppermute | solution.py:250
  186.8 18.0 %stats.2 = f32[4,4,20,256]{3,2,1,0:T(8,128)} custom-call(s32[48]{0:T(128)} %concatenate.73.table, bf16[4,256,2560]{2,1,0:T(8,128)(2,1)} %bitcast.69, bf16[2,112,5120]{2,1,0:T(8,128)(2,1)} %bitcast.74, bf16[2,112,5120]{2,1,0:T(8,128)(2,1)} %collective-permute-done.4.ks, bf16[5,112,5120]{2,1,0:T(8,128)(2,1)} %bitcast.58, bf16[5,112,5120]{2,1,0:T(8,128)(2,1)} %bitcast.59, ...), custom_call_target="tpu_custom_call" | custom-call | flops 1468006400 | bytes 18350080 | tf_op jit(solution)/shard_map/stats/pallas_call | solution.py:153
  206.1 5.9 %collective-permute-start.6 = (f32[4,4,20,64]{3,2,1,0:T(8,128)S(1)}, f32[4,4,20,64]{3,2,1,0:T(8,128)S(1)}, u32[]{:S(2)}, u32[]{:S(2)}) collective-permute-start(f32[4,4,20,64]{3,2,1,0:T(8,128)S(1)} %get-tuple-element.50), channel_id=1, source_target_pairs={{0,65},{1,66},{2,67},{3,68},{4,69},{5,70},{6,71},{7,72},{8,73},{9,... | collective-permute-start | bytes 245768 | tf_op jit(solution)/shard_map/ppermute | solution.py:247
  212.0 4.4 %collective-permute-start.7 = (f32[4,4,20,64]{3,2,1,0:T(8,128)S(1)}, f32[4,4,20,64]{3,2,1,0:T(8,128)S(1)}, u32[]{:S(2)}, u32[]{:S(2)}) collective-permute-start(f32[4,4,20,64]{3,2,1,0:T(8,128)S(1)} %get-tuple-element.49), channel_id=1, source_target_pairs={{1,64},{2,65},{3,66},{4,67},{5,68},{6,69},{7,70},{8,71},{9,72},{10... | collective-permute-start | bytes 245768 | tf_op jit(solution)/shard_map/ppermute | solution.py:250
  216.7 2.8 collective-permute-start.22
  221.0 1.8 collective-permute-start.8
  224.5 1.4 collective-permute-done.8
  226.2 1.6 collective-permute-start.9
  228.2 7.8 %collective-permute-start.25 = (f32[4,4,20,64]{3,2,1,0:T(8,128)S(1)}, f32[4,4,20,64]{3,2,1,0:T(8,128)S(1)}, u32[]{:S(2)}, u32[]{:S(2)}) collective-permute-start(f32[4,4,20,64]{3,2,1,0:T(8,128)S(1)} %get-tuple-element.64), channel_id=1, source_target_pairs={{1,64},{2,65},{3,66},{4,67},{5,68},{6,69},{7,70},{8,71},{9,72},{10... | collective-permute-start | bytes 245768 | tf_op jit(solution)/shard_map/ppermute | solution.py:250
  236.0 1.9 collective-permute-start.24
  238.1 8.1 %collective-permute-start.11 = (f32[4,4,20,64]{3,2,1,0:T(8,128)S(1)}, f32[4,4,20,64]{3,2,1,0:T(8,128)S(1)}, u32[]{:S(2)}, u32[]{:S(2)}) collective-permute-start(f32[4,4,20,64]{3,2,1,0:T(8,128)S(1)} %get-tuple-element.58), channel_id=1, source_target_pairs={{1,64},{2,65},{3,66},{4,67},{5,68},{6,69},{7,70},{8,71},{9,72},{10... | collective-permute-start | bytes 245768 | tf_op jit(solution)/shard_map/ppermute | solution.py:250
  246.2 1.9 collective-permute-start.10
  249.2 2.6 copy-done
  251.8 33.4 %output.3 = f32[4,4,56,2560]{3,2,1,0:T(8,128)} custom-call(s32[48]{0:T(128)} %concatenate.73.table, bf16[4,256,2560]{2,1,0:T(8,128)(2,1)} %bitcast.72, f32[4,4,20,256]{3,2,1,0:T(8,128)} %maximum_maximum_fusion.1.tot_ref, bf16[2,112,5120]{2,1,0:T(8,128)(2,1)} %bitcast.75, bf16[2,112,5120]{2,1,0:T(8,128)(2,1)} %collective-permute-done.4.ks, ...), custom_call_target="tpu_custom_call" | custom-call | flops 2936012800 | bytes 36700160 | tf_op jit(solution)/shard_map/output/pallas_call | solution.py:176
  285.2 1.7 fusion.62
  286.9 1.8 slice.517
  289.8 33.4 %output.2 = f32[4,4,56,2560]{3,2,1,0:T(8,128)} custom-call(s32[48]{0:T(128)} %concatenate.73.table, bf16[4,256,2560]{2,1,0:T(8,128)(2,1)} %bitcast.70, f32[4,4,20,256]{3,2,1,0:T(8,128)} %maximum_maximum_fusion.tot_ref, bf16[2,112,5120]{2,1,0:T(8,128)(2,1)} %bitcast.76, bf16[2,112,5120]{2,1,0:T(8,128)(2,1)} %collective-permute-done.4.ks, ...), custom_call_target="tpu_custom_call" | custom-call | flops 2936012800 | bytes 36700160 | tf_op jit(solution)/shard_map/output/pallas_call | solution.py:176
  323.2 2.6 slice_bitcast_fusion.1
  325.8 18.3 %collective-permute-start.15 = (bf16[4,56,2560]{2,1,0:T(8,128)(2,1)S(1)}, bf16[4,56,2560]{2,1,0:T(8,128)(2,1)S(1)}, u32[]{:S(2)}, u32[]{:S(2)}) collective-permute-start(bf16[4,56,2560]{2,1,0:T(8,128)(2,1)S(1)} %get-tuple-element.26), channel_id=1, source_target_pairs={{1,64},{2,65},{3,66},{4,67},{5,68},{6,69},{7,70},{8,71},{9,72},{10... | collective-permute-start | bytes 3440648 | tf_op jit(solution)/shard_map/ppermute | solution.py:250
  344.1 1.9 collective-permute-start.14
  346.6 22.0 %collective-permute-done.15 = bf16[4,56,2560]{2,1,0:T(8,128)(2,1)S(1)} collective-permute-done((bf16[4,56,2560]{2,1,0:T(8,128)(2,1)S(1)}, bf16[4,56,2560]{2,1,0:T(8,128)(2,1)S(1)}, u32[]{:S(2)}, u32[]{:S(2)}) %collective-permute-start.15) | collective-permute-done | bytes 1146912 | tf_op jit(solution)/shard_map/ppermute | solution.py:250
  368.6 13.0 %collective-permute-done.14 = bf16[4,56,2560]{2,1,0:T(8,128)(2,1)S(1)} collective-permute-done((bf16[4,56,2560]{2,1,0:T(8,128)(2,1)S(1)}, bf16[4,56,2560]{2,1,0:T(8,128)(2,1)S(1)}, u32[]{:S(2)}, u32[]{:S(2)}) %collective-permute-start.14) | collective-permute-done | bytes 1146912 | tf_op jit(solution)/shard_map/ppermute | solution.py:247
  382.3 15.6 %collective-permute-done.26 = bf16[2,4,56,2560]{3,2,0,1:T(8,128)(2,1)S(1)} collective-permute-done((bf16[2,4,56,2560]{3,2,0,1:T(8,128)(2,1)S(1)}, bf16[2,4,56,2560]{3,2,0,1:T(8,128)(2,1)S(1)}, u32[]{:S(2)}, u32[]{:S(2)}) %collective-permute-start.26) | collective-permute-done | bytes 2293792 | tf_op jit(solution)/shard_map/ppermute | solution.py:244
  397.9 1.4 fusion.25
  399.3 7.9 %collective-permute-start.28 = (bf16[2,56,2560]{2,1,0:T(8,128)(2,1)S(1)}, bf16[2,56,2560]{2,1,0:T(8,128)(2,1)S(1)}, u32[]{:S(2)}, u32[]{:S(2)}) collective-permute-start(bf16[2,56,2560]{2,1,0:T(8,128)(2,1)S(1)} %fusion.25), channel_id=1, source_target_pairs={{1,64},{2,65},{3,66},{4,67},{5,68},{6,69},{7,70},{8,71},{9,72},{10... | collective-permute-start | bytes 1720328 | tf_op jit(solution)/shard_map/ppermute | solution.py:250
  407.1 1.4 fusion.24
  408.5 1.9 collective-permute-start.27
  410.9 3.4 collective-permute-done.28
  414.3 10.0 %collective-permute-done.27 = bf16[2,56,2560]{2,1,0:T(8,128)(2,1)S(1)} collective-permute-done((bf16[2,56,2560]{2,1,0:T(8,128)(2,1)S(1)}, bf16[2,56,2560]{2,1,0:T(8,128)(2,1)S(1)}, u32[]{:S(2)}, u32[]{:S(2)}) %collective-permute-start.27) | collective-permute-done | bytes 573472 | tf_op jit(solution)/shard_map/ppermute | solution.py:247
  424.3 2.0 fusion.15
  426.6 1.6 copy.63
  (113 shorter events, 15.5 us)
Async XLA Ops:
  0.0 12.6 %copy-start.1 = (bf16[2,2,56,5120]{3,2,1,0:T(8,128)(2,1)S(1)}, bf16[2,2,56,5120]{3,2,1,0:T(8,128)(2,1)}, u32[]{:S(2)}) copy-start(bf16[2,2,56,5120]{3,2,1,0:T(8,128)(2,1)} %param.13) | copy-start | bytes 6881284
  0.0 49.1 %collective-permute-start = (s32[2,2]{1,0:T(2,128)}, s32[2,2]{1,0:T(2,128)S(1)}, u32[]{:S(2)}, u32[]{:S(2)}) collective-permute-start(s32[2,2]{1,0:T(2,128)} %param.15), channel_id=1, source_target_pairs={{0,32},{1,33},{2,34},{3,35},{4,36},{5,37},{6,38},{7,39},{8,40},{9,... | collective-permute-start | bytes 56 | tf_op jit(solution)/shard_map/ppermute | solution.py:241
  2.5 47.5 %collective-permute-start.17 = (bf16[2,56,2560]{2,1,0:T(8,128)(2,1)}, bf16[2,56,2560]{2,1,0:T(8,128)(2,1)S(1)}, u32[]{:S(2)}, u32[]{:S(2)}) collective-permute-start(bf16[2,56,2560]{2,1,0:T(8,128)(2,1)} %get-tuple-element.35), channel_id=1, source_target_pairs={{0,65},{1,66},{2,67},{3,68},{4,69},{5,70},{6,71},{7,72},{8,73},{9,... | collective-permute-start | bytes 1720328 | tf_op jit(solution)/shard_map/ppermute | solution.py:247
  7.2 43.3 %collective-permute-start.18 = (bf16[2,56,2560]{2,1,0:T(8,128)(2,1)}, bf16[2,56,2560]{2,1,0:T(8,128)(2,1)}, u32[]{:S(2)}, u32[]{:S(2)}) collective-permute-start(bf16[2,56,2560]{2,1,0:T(8,128)(2,1)} %get-tuple-element.36), channel_id=1, source_target_pairs={{1,64},{2,65},{3,66},{4,67},{5,68},{6,69},{7,70},{8,71},{9,72},{10... | collective-permute-start | bytes 1720328 | tf_op jit(solution)/shard_map/ppermute | solution.py:250
  12.6 3.7 copy-start.11
  12.6 3.8 copy-start.8
  12.6 3.8 copy-start.10
  12.6 143.7 %collective-permute-start.4 = (bf16[2,112,5120]{2,1,0:T(8,128)(2,1)S(1)}, bf16[2,112,5120]{2,1,0:T(8,128)(2,1)}, u32[]{:S(2)}, u32[]{:S(2)}) collective-permute-start(bf16[2,112,5120]{2,1,0:T(8,128)(2,1)S(1)} %bitcast.77), channel_id=1, source_target_pairs={{0,32},{1,33},{2,34},{3,35},{4,36},{5,37},{6,38},{7,39},{8,40},{9,... | collective-permute-start | bytes 6881288 | tf_op jit(solution)/shard_map/ppermute | solution.py:241
  16.0 28.0 %collective-permute-start.1 = (bf16[2,2,56,2560]{3,2,1,0:T(8,128)(2,1)}, bf16[2,2,56,2560]{3,2,1,0:T(8,128)(2,1)}, u32[]{:S(2)}, u32[]{:S(2)}) collective-permute-start(bf16[2,2,56,2560]{3,2,1,0:T(8,128)(2,1)} %get-tuple-element.31), channel_id=1, source_target_pairs={{0,64},{1,65},{2,66},{3,67},{4,68},{5,69},{6,70},{7,71},{8,72},{9,... | collective-permute-start | bytes 3440648 | tf_op jit(solution)/shard_map/ppermute | solution.py:244
  17.7 31.6 %copy-start.9 = (s32[2,2]{1,0:T(2,128)S(1)}, s32[2,2]{1,0:T(2,128)}, u32[]{:S(2)}) copy-start(s32[2,2]{1,0:T(2,128)} %param.15) | copy-start | bytes 52
  47.1 34.6 %collective-permute-start.2 = (bf16[4,56,2560]{2,1,0:T(8,128)(2,1)}, bf16[4,56,2560]{2,1,0:T(8,128)(2,1)}, u32[]{:S(2)}, u32[]{:S(2)}) collective-permute-start(bf16[4,56,2560]{2,1,0:T(8,128)(2,1)} %get-tuple-element.29), channel_id=1, source_target_pairs={{0,65},{1,66},{2,67},{3,68},{4,69},{5,70},{6,71},{7,72},{8,73},{9,... | collective-permute-start | bytes 3440648 | tf_op jit(solution)/shard_map/ppermute | solution.py:247
  49.1 107.2 %collective-permute-start.5 = (bf16[5,112,5120]{2,1,0:T(8,128)(2,1)}, bf16[5,112,5120]{2,1,0:T(8,128)(2,1)}, u32[]{:S(2)}, u32[]{:S(2)}) collective-permute-start(bf16[5,112,5120]{2,1,0:T(8,128)(2,1)} %bitcast.55), channel_id=1, source_target_pairs={{0,32},{1,33},{2,34},{3,35},{4,36},{5,37},{6,38},{7,39},{8,40},{9,... | collective-permute-start | bytes 17203208 | tf_op jit(solution)/shard_map/ppermute | solution.py:241
  50.0 10.3 %copy-start.6 = (bf16[2,56,2560]{2,1,0:T(8,128)(2,1)}, bf16[2,56,2560]{2,1,0:T(8,128)(2,1)S(1)}, u32[]{:S(2)}) copy-start(bf16[2,56,2560]{2,1,0:T(8,128)(2,1)S(1)} %collective-permute-done.17) | copy-start | bytes 1720324
  50.0 199.2 %collective-permute-start.12 = (bf16[2,112,5120]{2,1,0:T(8,128)(2,1)}, bf16[2,112,5120]{2,1,0:T(8,128)(2,1)}, u32[]{:S(2)}, u32[]{:S(2)}) collective-permute-start(bf16[2,112,5120]{2,1,0:T(8,128)(2,1)} %bitcast.78), channel_id=1, source_target_pairs={{0,32},{1,33},{2,34},{3,35},{4,36},{5,37},{6,38},{7,39},{8,40},{9,... | collective-permute-start | bytes 6881288 | tf_op jit(solution)/shard_map/ppermute | solution.py:241
  50.5 50.6 %collective-permute-start.3 = (bf16[4,56,2560]{2,1,0:T(8,128)(2,1)}, bf16[4,56,2560]{2,1,0:T(8,128)(2,1)S(1)}, u32[]{:S(2)}, u32[]{:S(2)}) collective-permute-start(bf16[4,56,2560]{2,1,0:T(8,128)(2,1)} %get-tuple-element.30), channel_id=1, source_target_pairs={{1,64},{2,65},{3,66},{4,67},{5,68},{6,69},{7,70},{8,71},{9,72},{10... | collective-permute-start | bytes 3440648 | tf_op jit(solution)/shard_map/ppermute | solution.py:250
  81.7 167.5 %collective-permute-start.13 = (bf16[5,112,5120]{2,1,0:T(8,128)(2,1)}, bf16[5,112,5120]{2,1,0:T(8,128)(2,1)S(1)}, u32[]{:S(2)}, u32[]{:S(2)}) collective-permute-start(bf16[5,112,5120]{2,1,0:T(8,128)(2,1)} %bitcast.64), channel_id=1, source_target_pairs={{0,32},{1,33},{2,34},{3,35},{4,36},{5,37},{6,38},{7,39},{8,40},{9,... | collective-permute-start | bytes 17203208 | tf_op jit(solution)/shard_map/ppermute | solution.py:241
  101.1 50.6 %collective-permute-start.19 = (bf16[2,4,56,2560]{3,2,0,1:T(8,128)(2,1)S(1)}, bf16[2,4,56,2560]{3,2,0,1:T(8,128)(2,1)S(1)}, u32[]{:S(2)}, u32[]{:S(2)}) collective-permute-start(bf16[2,4,56,2560]{3,2,0,1:T(8,128)(2,1)S(1)} %pad_maximum_fusion), channel_id=1, source_target_pairs={{0,64},{1,65},{2,66},{3,67},{4,68},{5,69},{6,70},{7,71},{8,72},{9,... | collective-permute-start | bytes 6881288 | tf_op jit(solution)/shard_map/ppermute | solution.py:244
  105.9 45.8 %copy-start.7 = (bf16[2,56,2560]{2,1,0:T(8,128)(2,1)S(1)}, bf16[2,56,2560]{2,1,0:T(8,128)(2,1)}, u32[]{:S(2)}) copy-start(bf16[2,56,2560]{2,1,0:T(8,128)(2,1)} %copy-done.6) | copy-start | bytes 1720324
  151.8 1.4 copy-start.3
  175.4 36.6 %collective-permute-start.20 = (f32[4,4,20,64]{3,2,1,0:T(8,128)S(1)}, f32[4,4,20,64]{3,2,1,0:T(8,128)S(1)}, u32[]{:S(2)}, u32[]{:S(2)}) collective-permute-start(f32[4,4,20,64]{3,2,1,0:T(8,128)S(1)} %get-tuple-element.54), channel_id=1, source_target_pairs={{0,65},{1,66},{2,67},{3,68},{4,69},{5,70},{6,71},{7,72},{8,73},{9,... | collective-permute-start | bytes 245768 | tf_op jit(solution)/shard_map/ppermute | solution.py:247
  182.4 34.0 %collective-permute-start.21 = (f32[4,4,20,64]{3,2,1,0:T(8,128)S(1)}, f32[4,4,20,64]{3,2,1,0:T(8,128)S(1)}, u32[]{:S(2)}, u32[]{:S(2)}) collective-permute-start(f32[4,4,20,64]{3,2,1,0:T(8,128)S(1)} %get-tuple-element.53), channel_id=1, source_target_pairs={{1,64},{2,65},{3,66},{4,67},{5,68},{6,69},{7,70},{8,71},{9,72},{10... | collective-permute-start | bytes 245768 | tf_op jit(solution)/shard_map/ppermute | solution.py:250
  186.8 29.7 %copy-start.5 = (f32[4,4,20,256]{3,2,1,0:T(8,128)S(1)}, f32[4,4,20,256]{3,2,1,0:T(8,128)}, u32[]{:S(2)}) copy-start(f32[4,4,20,256]{3,2,1,0:T(8,128)} %stats.3) | copy-start | bytes 983044
  204.9 16.0 %copy-start.4 = (f32[4,4,20,256]{3,2,1,0:T(8,128)S(1)}, f32[4,4,20,256]{3,2,1,0:T(8,128)}, u32[]{:S(2)}) copy-start(f32[4,4,20,256]{3,2,1,0:T(8,128)} %stats.2) | copy-start | bytes 983044
  206.1 13.4 %collective-permute-start.6 = (f32[4,4,20,64]{3,2,1,0:T(8,128)S(1)}, f32[4,4,20,64]{3,2,1,0:T(8,128)S(1)}, u32[]{:S(2)}, u32[]{:S(2)}) collective-permute-start(f32[4,4,20,64]{3,2,1,0:T(8,128)S(1)} %get-tuple-element.50), channel_id=1, source_target_pairs={{0,65},{1,66},{2,67},{3,68},{4,69},{5,70},{6,71},{7,72},{8,73},{9,... | collective-permute-start | bytes 245768 | tf_op jit(solution)/shard_map/ppermute | solution.py:247
  212.0 8.8 %collective-permute-start.7 = (f32[4,4,20,64]{3,2,1,0:T(8,128)S(1)}, f32[4,4,20,64]{3,2,1,0:T(8,128)S(1)}, u32[]{:S(2)}, u32[]{:S(2)}) collective-permute-start(f32[4,4,20,64]{3,2,1,0:T(8,128)S(1)} %get-tuple-element.49), channel_id=1, source_target_pairs={{1,64},{2,65},{3,66},{4,67},{5,68},{6,69},{7,70},{8,71},{9,72},{10... | collective-permute-start | bytes 245768 | tf_op jit(solution)/shard_map/ppermute | solution.py:250
  216.7 6.3 %collective-permute-start.22 = (f32[2,4,20,128]{3,2,1,0:T(8,128)S(1)}, f32[2,4,20,128]{3,2,1,0:T(8,128)S(1)}, u32[]{:S(2)}, u32[]{:S(2)}) collective-permute-start(f32[2,4,20,128]{3,2,1,0:T(8,128)S(1)} %pad_maximum_fusion.8), channel_id=1, source_target_pairs={{0,64},{1,65},{2,66},{3,67},{4,68},{5,69},{6,70},{7,71},{8,72},{9,... | collective-permute-start | bytes 245768 | tf_op jit(solution)/shard_map/ppermute | solution.py:244
  221.0 4.9 %collective-permute-start.8 = (f32[2,4,20,128]{3,2,1,0:T(8,128)S(1)}, f32[2,4,20,128]{3,2,1,0:T(8,128)S(1)}, u32[]{:S(2)}, u32[]{:S(2)}) collective-permute-start(f32[2,4,20,128]{3,2,1,0:T(8,128)S(1)} %pad_maximum_fusion.6), channel_id=1, source_target_pairs={{0,64},{1,65},{2,66},{3,67},{4,68},{5,69},{6,70},{7,71},{8,72},{9,... | collective-permute-start | bytes 245768 | tf_op jit(solution)/shard_map/ppermute | solution.py:244
  223.3 4.7 %collective-permute-start.23 = (f32[2,4,20,128]{3,2,1,0:T(8,128)S(1)}, f32[2,4,20,128]{3,2,1,0:T(8,128)S(1)}, u32[]{:S(2)}, u32[]{:S(2)}) collective-permute-start(f32[2,4,20,128]{3,2,1,0:T(8,128)S(1)} %pad_maximum_fusion.9), channel_id=1, source_target_pairs={{0,64},{1,65},{2,66},{3,67},{4,68},{5,69},{6,70},{7,71},{8,72},{9,... | collective-permute-start | bytes 245768 | tf_op jit(solution)/shard_map/ppermute | solution.py:244
  226.2 11.7 %collective-permute-start.9 = (f32[2,4,20,128]{3,2,1,0:T(8,128)S(1)}, f32[2,4,20,128]{3,2,1,0:T(8,128)S(1)}, u32[]{:S(2)}, u32[]{:S(2)}) collective-permute-start(f32[2,4,20,128]{3,2,1,0:T(8,128)S(1)} %pad_maximum_fusion.7), channel_id=1, source_target_pairs={{0,64},{1,65},{2,66},{3,67},{4,68},{5,69},{6,70},{7,71},{8,72},{9,... | collective-permute-start | bytes 245768 | tf_op jit(solution)/shard_map/ppermute | solution.py:244
  228.2 18.1 %collective-permute-start.25 = (f32[4,4,20,64]{3,2,1,0:T(8,128)S(1)}, f32[4,4,20,64]{3,2,1,0:T(8,128)S(1)}, u32[]{:S(2)}, u32[]{:S(2)}) collective-permute-start(f32[4,4,20,64]{3,2,1,0:T(8,128)S(1)} %get-tuple-element.64), channel_id=1, source_target_pairs={{1,64},{2,65},{3,66},{4,67},{5,68},{6,69},{7,70},{8,71},{9,72},{10... | collective-permute-start | bytes 245768 | tf_op jit(solution)/shard_map/ppermute | solution.py:250
  236.0 12.2 %collective-permute-start.24 = (f32[4,4,20,64]{3,2,1,0:T(8,128)S(1)}, f32[4,4,20,64]{3,2,1,0:T(8,128)S(1)}, u32[]{:S(2)}, u32[]{:S(2)}) collective-permute-start(f32[4,4,20,64]{3,2,1,0:T(8,128)S(1)} %get-tuple-element.63), channel_id=1, source_target_pairs={{0,65},{1,66},{2,67},{3,68},{4,69},{5,70},{6,71},{7,72},{8,73},{9,... | collective-permute-start | bytes 245768 | tf_op jit(solution)/shard_map/ppermute | solution.py:247
  238.1 48.8 %collective-permute-start.11 = (f32[4,4,20,64]{3,2,1,0:T(8,128)S(1)}, f32[4,4,20,64]{3,2,1,0:T(8,128)S(1)}, u32[]{:S(2)}, u32[]{:S(2)}) collective-permute-start(f32[4,4,20,64]{3,2,1,0:T(8,128)S(1)} %get-tuple-element.58), channel_id=1, source_target_pairs={{1,64},{2,65},{3,66},{4,67},{5,68},{6,69},{7,70},{8,71},{9,72},{10... | collective-permute-start | bytes 245768 | tf_op jit(solution)/shard_map/ppermute | solution.py:250
  246.2 42.6 %collective-permute-start.10 = (f32[4,4,20,64]{3,2,1,0:T(8,128)S(1)}, f32[4,4,20,64]{3,2,1,0:T(8,128)S(1)}, u32[]{:S(2)}, u32[]{:S(2)}) collective-permute-start(f32[4,4,20,64]{3,2,1,0:T(8,128)S(1)} %get-tuple-element.57), channel_id=1, source_target_pairs={{0,65},{1,66},{2,67},{3,68},{4,69},{5,70},{6,71},{7,72},{8,73},{9,... | collective-permute-start | bytes 245768 | tf_op jit(solution)/shard_map/ppermute | solution.py:247
  249.2 2.6 copy-start
  325.8 42.8 %collective-permute-start.15 = (bf16[4,56,2560]{2,1,0:T(8,128)(2,1)S(1)}, bf16[4,56,2560]{2,1,0:T(8,128)(2,1)S(1)}, u32[]{:S(2)}, u32[]{:S(2)}) collective-permute-start(bf16[4,56,2560]{2,1,0:T(8,128)(2,1)S(1)} %get-tuple-element.26), channel_id=1, source_target_pairs={{1,64},{2,65},{3,66},{4,67},{5,68},{6,69},{7,70},{8,71},{9,72},{10... | collective-permute-start | bytes 3440648 | tf_op jit(solution)/shard_map/ppermute | solution.py:250
  344.1 37.5 %collective-permute-start.14 = (bf16[4,56,2560]{2,1,0:T(8,128)(2,1)S(1)}, bf16[4,56,2560]{2,1,0:T(8,128)(2,1)S(1)}, u32[]{:S(2)}, u32[]{:S(2)}) collective-permute-start(bf16[4,56,2560]{2,1,0:T(8,128)(2,1)S(1)} %get-tuple-element.25), channel_id=1, source_target_pairs={{0,65},{1,66},{2,67},{3,68},{4,69},{5,70},{6,71},{7,72},{8,73},{9,... | collective-permute-start | bytes 3440648 | tf_op jit(solution)/shard_map/ppermute | solution.py:247
  346.0 35.9 %copy-start.2 = (f32[4,4,56,2560]{3,2,1,0:T(8,128)S(1)}, f32[4,4,56,2560]{3,2,1,0:T(8,128)}, u32[]{:S(2)}) copy-start(f32[4,4,56,2560]{3,2,1,0:T(8,128)} %output.2) | copy-start | bytes 27525124
  346.3 51.6 %collective-permute-start.26 = (bf16[2,4,56,2560]{3,2,0,1:T(8,128)(2,1)S(1)}, bf16[2,4,56,2560]{3,2,0,1:T(8,128)(2,1)S(1)}, u32[]{:S(2)}, u32[]{:S(2)}) collective-permute-start(bf16[2,4,56,2560]{3,2,0,1:T(8,128)(2,1)S(1)} %pad_maximum_fusion.1), channel_id=1, source_target_pairs={{0,64},{1,65},{2,66},{3,67},{4,68},{5,69},{6,70},{7,71},{8,72},{9,... | collective-permute-start | bytes 6881288 | tf_op jit(solution)/shard_map/ppermute | solution.py:244
  382.2 28.2 %collective-permute-start.16 = (bf16[2,2,56,2560]{3,2,0,1:T(8,128)(2,1)S(1)}, bf16[2,2,56,2560]{3,2,0,1:T(8,128)(2,1)S(1)}, u32[]{:S(2)}, u32[]{:S(2)}) collective-permute-start(bf16[2,2,56,2560]{3,2,0,1:T(8,128)(2,1)S(1)} %fusion.16), channel_id=1, source_target_pairs={{0,64},{1,65},{2,66},{3,67},{4,68},{5,69},{6,70},{7,71},{8,72},{9,... | collective-permute-start | bytes 3440648 | tf_op jit(solution)/shard_map/ppermute | solution.py:244
  399.3 15.1 %collective-permute-start.28 = (bf16[2,56,2560]{2,1,0:T(8,128)(2,1)S(1)}, bf16[2,56,2560]{2,1,0:T(8,128)(2,1)S(1)}, u32[]{:S(2)}, u32[]{:S(2)}) collective-permute-start(bf16[2,56,2560]{2,1,0:T(8,128)(2,1)S(1)} %fusion.25), channel_id=1, source_target_pairs={{1,64},{2,65},{3,66},{4,67},{5,68},{6,69},{7,70},{8,71},{9,72},{10... | collective-permute-start | bytes 1720328 | tf_op jit(solution)/shard_map/ppermute | solution.py:250
  408.5 15.8 %collective-permute-start.27 = (bf16[2,56,2560]{2,1,0:T(8,128)(2,1)S(1)}, bf16[2,56,2560]{2,1,0:T(8,128)(2,1)S(1)}, u32[]{:S(2)}, u32[]{:S(2)}) collective-permute-start(bf16[2,56,2560]{2,1,0:T(8,128)(2,1)S(1)} %fusion.24), channel_id=1, source_target_pairs={{0,65},{1,66},{2,67},{3,68},{4,69},{5,70},{6,71},{7,72},{8,73},{9,... | collective-permute-start | bytes 1720328 | tf_op jit(solution)/shard_map/ppermute | solution.py:247
